TPU v7x, 512 devices: a whole 4x4x16 slice. The times are simulated.
512 devices in a mesh: cube: 8 (over x, core), front: 64 (over z, y).
Axes of the slice: x: 4, y: 4, z: 16, core: 2. Of those that a mesh axis runs over, the one named last changes fastest.
Arguments:
- leaf_blocks: float32 [8, 3840, 3840], P('cube', 'front'), may hold values from -8 to 11, as said below
- front_entries: float32 [7, 4096, 256], P(None, 'front'), may hold values from -0.001 to 3
- child_maps: int32 [7, 2, 60], replicated, may hold values from 0 to 63, as said below
Outputs:
- factor_columns: float32 [8, 3, 4096, 256], P('cube', None, 'front')
- top_block: float32 [3840, 3840], P('front')
Inputs may be any that keep to these rules, and one draw needn't show every extreme that they name: `child_maps`: for each node, each of the two rows lists distinct offsets, and the two rows together name every offset from 0 to 63. `leaf_blocks`: each leaf block is symmetric positive definite.
All inputs are finite; a program needn't handle non-finite values.
Results may differ from a plain program's by a relative error of at most 0.00033.
Values may be sent and summed in bfloat16 or wider, within the bound.
No kernel may reach another device: no remote copies, remote signals or barrier semaphores. Data moves between devices by JAX's collectives and lax.ppermute only.
A program may use at most 128 MiB of HBM per device.

v0:
```python
import jax
import jax.numpy as jnp
from jax import lax
from jax.sharding import PartitionSpec as P

PANEL = 256
HIGH = lax.Precision.HIGHEST


def swapped(value, axis, apart):
    mask = 2**apart
    pairs = [(source, source ^ mask) for source in range(lax.axis_size(axis))]
    return lax.ppermute(value, axis, pairs)


def onehot_table(mapping, width):
    return (mapping[:, None] == jnp.arange(width, dtype=jnp.int32)[None, :]).astype(jnp.float32)


def scatter_rows(block, mapping, devices, width):
    block_rows = block.shape[0]
    table = onehot_table(mapping, width)
    grid = block.reshape(block_rows, devices, block_rows)
    widened = jnp.einsum("ubv,vs->usb", grid, table, precision=HIGH)
    placed = jnp.einsum("usb,ut->tsb", widened, table, precision=HIGH)
    return placed.reshape(width, width * devices)


def cholesky_lower(pivot):
    symmetric = jnp.tril(pivot) + jnp.tril(pivot, -1).T
    return jnp.linalg.cholesky(symmetric)


def factor_front(matrix, devices, position, width, panel_rows):
    panel = panel_rows * devices
    trailing = width - panel_rows
    last_col = panel_rows * devices
    local_pivot = matrix[0:panel_rows, 0:last_col]
    gathered = lax.all_gather(local_pivot, "front", axis=0, tiled=True)
    pivot = jnp.transpose(gathered.reshape(devices, panel_rows, panel), (1, 0, 2)).reshape(
        panel, panel
    )
    factor = cholesky_lower(pivot)
    lhs_rows = matrix[panel_rows:, 0:last_col]
    solved = jax.scipy.linalg.solve_triangular(factor, lhs_rows.T, lower=True).T
    rounded = solved.astype(jnp.bfloat16)
    update = jnp.einsum(
        "ip,jp->ij",
        rounded,
        lax.all_gather(rounded, "front", axis=0, tiled=True),
        preferred_element_type=jnp.float32,
    )
    reordered = jnp.transpose(update.reshape(trailing, devices, trailing), (0, 2, 1)).reshape(
        trailing, trailing * devices
    )
    matrix = matrix.at[panel_rows:, last_col:].add(-reordered)
    upper = jnp.zeros((0, panel), jnp.float32)
    middle = lax.dynamic_index_in_dim(
        factor.reshape(panel_rows, devices, panel), position, 1, keepdims=False
    )
    columns = jnp.concatenate([upper, middle, solved], axis=0)
    return (columns, matrix)


def on_device(leaf_blocks, front_entries, child_maps):
    devices = lax.axis_size("front")
    position = lax.axis_index("front")
    subcube = lax.axis_index("cube")
    cube_count = lax.axis_size("cube")
    heights = cube_count.bit_length() - 1
    width = front_entries.shape[1]
    sep_rows = front_entries.shape[2] // devices
    panel_rows = PANEL // devices
    block_rows = leaf_blocks.shape[1]
    current = leaf_blocks[0]
    factors = []
    for height in range(heights):
        sibling = swapped(current, "cube", height)
        side_bit = jnp.right_shift(subcube, height) & 1
        left_block = jnp.where(side_bit == 0, current, sibling)
        right_block = jnp.where(side_bit == 0, sibling, current)
        node = jnp.right_shift(subcube + cube_count, height + 1)
        entries = lax.dynamic_index_in_dim(front_entries, node - 1, 0, keepdims=False)
        mappings = lax.dynamic_index_in_dim(child_maps, node - 1, 0, keepdims=False)
        placed_entries = jnp.transpose(
            entries.reshape(width, devices, sep_rows), (0, 2, 1)
        ).reshape(width, sep_rows * devices)
        zeros_rest = jnp.zeros((width, (width - sep_rows) * devices), jnp.float32)
        matrix = jnp.concatenate([placed_entries, zeros_rest], axis=1)
        matrix = matrix + scatter_rows(left_block, mappings[0], devices, width)
        matrix = matrix + scatter_rows(right_block, mappings[1], devices, width)
        factor_part, matrix = factor_front(matrix, devices, position, width, panel_rows)
        factors.append(factor_part)
        remain = matrix[sep_rows:, sep_rows * devices :].reshape(block_rows, block_rows, devices)
        current = jnp.transpose(remain, (0, 2, 1)).reshape(block_rows, devices * block_rows)
    return (jnp.stack(factors)[None], current)


def solution(mesh):
    in_specs = (P("cube", "front", None), P(None, "front", None), P())
    out_specs = (P("cube", None, "front", None), P("front", None))
    return jax.shard_map(
        on_device, mesh=mesh, in_specs=in_specs, out_specs=out_specs, check_vma=False
    )
```

profile of v0, /device:TPU:2, one launch (start us, length us, event | category | flops | bytes accessed | tf_op | source)
XLA Modules:
  0.0 1041.9 jit_solution(18427782496393358375)
XLA Ops:
  8.5 1.9 collective-permute-start
  14.8 4.3 reshape.238
  19.1 2.9 convolution_bitcast_fusion.5
  22.0 2.4 fusion.10
  27.4 2.9 reshape.240
  30.3 2.9 convolution_bitcast_fusion.4
  33.2 2.9 fusion.8
  40.7 88.9 %all-gather = f32[64,4,256]{2,1,0:T(4,128)S(1)} all-gather(f32[1,4,256]{2,1,0:T(4,128)S(1)} %slice_bitcast_fusion.17), channel_id=1, replica_groups=mesh['cube'=8,'front'=64] {'front'}, dimensions={0}, use_global_device_ids=true | all-gather | bytes 266240 | tf_op jit(solution)/shard_map/all_gather | solution.py:39
  130.1 11.7 %cholesky.172 = f32[128,128]{1,0:T(8,128)S(1)} custom-call(f32[128,128]{1,0:T(8,128)S(1)} %copy.109), custom_call_target="Cholesky" | custom-call | tf_op jit(solution)/shard_map/jit(cholesky)/cholesky | solution.py:31
  141.9 9.8 custom-call.15
  152.4 11.7 %cholesky.189 = f32[128,128]{1,0:T(8,128)S(1)} custom-call(f32[128,128]{1,0:T(8,128)S(1)} %copy.111), custom_call_target="Cholesky" | custom-call | tf_op jit(solution)/shard_map/jit(cholesky)/cholesky | solution.py:31
  166.1 4.0 while.9
  170.1 19.7 %custom-call.16 = f32[2,128,128]{1,2,0:T(8,128)S(1)} custom-call(f32[2,128,128]{2,1,0:T(8,128)S(1)} %get-tuple-element.60), custom_call_target="InvertDiagBlocksLowerTriangular" | custom-call | tf_op jit(solution)/shard_map/jit(_solve_triangular)/triangular_solve | solution.py:45
  191.1 136.6 %all-gather.10.cloned.1.call-done = bf16[64,60,256]{2,1,0:T(8,128)(2,1)} async-done(((bf16[1,60,256]{2,1,0:T(8,128)(2,1)}), bf16[64,60,256]{2,1,0:T(8,128)(2,1)}) %all-gather.10.cloned.1.call-update) | async-done | bytes 1966096 | tf_op jit(solution)/shard_map/all_gather | solution.py:50
  327.7 2.5 reshape.297
  331.9 4.1 neg.37
  335.9 1.9 copy.114
  337.9 2.1 neg.39
  341.0 2.0 reshape.247
  343.0 1.9 copy.115
  344.9 2.8 reshape.248
  347.8 2.5 collective-permute-start.1
  350.6 13.7 %collective-permute-done.1 = f32[60,3840]{1,0:T(8,128)S(1)} collective-permute-done((f32[60,3840]{1,0:T(8,128)S(1)}, f32[60,3840]{1,0:T(8,128)S(1)}, u32[]{:S(2)}, u32[]{:S(2)}) %collective-permute-start.1) | collective-permute-done | bytes 921632 | tf_op jit(solution)/shard_map/ppermute | solution.py:13
  365.3 4.5 reshape.249
  369.8 2.9 convolution_bitcast_fusion.3
  372.7 2.4 fusion.6
  378.1 2.9 reshape.251
  381.0 2.9 convolution_bitcast_fusion.2
  383.9 2.6 fusion.4
  391.1 80.7 %all-gather.2 = f32[64,4,256]{2,1,0:T(4,128)S(1)} all-gather(f32[1,4,256]{2,1,0:T(4,128)S(1)} %slice_bitcast_fusion.16), channel_id=1, replica_groups=mesh['cube'=8,'front'=64] {'front'}, dimensions={0}, use_global_device_ids=true | all-gather | bytes 266240 | tf_op jit(solution)/shard_map/all_gather | solution.py:39
  472.3 11.7 %cholesky.206 = f32[128,128]{1,0:T(8,128)S(1)} custom-call(f32[128,128]{1,0:T(8,128)S(1)} %copy.124), custom_call_target="Cholesky" | custom-call | tf_op jit(solution)/shard_map/jit(cholesky)/cholesky | solution.py:31
  484.7 9.8 custom-call.17
  495.2 11.7 %cholesky.223 = f32[128,128]{1,0:T(8,128)S(1)} custom-call(f32[128,128]{1,0:T(8,128)S(1)} %copy.126), custom_call_target="Cholesky" | custom-call | tf_op jit(solution)/shard_map/jit(cholesky)/cholesky | solution.py:31
  509.6 4.2 while.10
  513.8 19.7 %custom-call.18 = f32[2,128,128]{1,2,0:T(8,128)S(1)} custom-call(f32[2,128,128]{2,1,0:T(8,128)S(1)} %get-tuple-element.61), custom_call_target="InvertDiagBlocksLowerTriangular" | custom-call | tf_op jit(solution)/shard_map/jit(_solve_triangular)/triangular_solve | solution.py:45
  534.8 135.8 %all-gather.12.cloned.1.call-done = bf16[64,60,256]{2,1,0:T(8,128)(2,1)} async-done(((bf16[1,60,256]{2,1,0:T(8,128)(2,1)}), bf16[64,60,256]{2,1,0:T(8,128)(2,1)}) %all-gather.12.cloned.1.call-update) | async-done | bytes 1966096 | tf_op jit(solution)/shard_map/all_gather | solution.py:50
  670.7 2.5 reshape.301
  674.8 4.1 neg.41
  678.9 1.9 copy.129
  680.8 2.1 neg.43
  684.0 2.0 reshape.258
  686.0 1.9 copy.130
  687.9 2.9 reshape.259
  690.7 4.0 collective-permute-start.2
  695.9 12.8 %collective-permute-done.2 = f32[60,3840]{1,0:T(8,128)S(1)} collective-permute-done((f32[60,3840]{1,0:T(8,128)S(1)}, f32[60,3840]{1,0:T(8,128)S(1)}, u32[]{:S(2)}, u32[]{:S(2)}) %collective-permute-start.2) | collective-permute-done | bytes 921632 | tf_op jit(solution)/shard_map/ppermute | solution.py:13
  709.8 4.2 reshape.260
  714.1 2.9 convolution_bitcast_fusion.1
  717.0 2.4 fusion.2
  722.3 2.9 reshape.262
  725.2 2.9 convolution_bitcast_fusion
  728.2 2.6 fusion
  735.4 80.7 %all-gather.4 = f32[64,4,256]{2,1,0:T(4,128)S(1)} all-gather(f32[1,4,256]{2,1,0:T(4,128)S(1)} %slice_bitcast_fusion.15), channel_id=1, replica_groups=mesh['cube'=8,'front'=64] {'front'}, dimensions={0}, use_global_device_ids=true | all-gather | bytes 266240 | tf_op jit(solution)/shard_map/all_gather | solution.py:39
  816.6 11.7 %cholesky.240 = f32[128,128]{1,0:T(8,128)S(1)} custom-call(f32[128,128]{1,0:T(8,128)S(1)} %cholesky.276), custom_call_target="Cholesky" | custom-call | tf_op jit(solution)/shard_map/jit(cholesky)/cholesky | solution.py:31
  829.0 9.8 custom-call.19
  839.3 11.7 %cholesky.257 = f32[128,128]{1,0:T(8,128)S(1)} custom-call(f32[128,128]{1,0:T(8,128)S(1)} %convolution_subtract_fusion), custom_call_target="Cholesky" | custom-call | tf_op jit(solution)/shard_map/jit(cholesky)/cholesky | solution.py:31
  853.1 4.3 while.11
  857.3 19.7 %custom-call.20 = f32[2,128,128]{1,2,0:T(8,128)S(1)} custom-call(f32[2,128,128]{2,1,0:T(8,128)S(1)} %get-tuple-element.62), custom_call_target="InvertDiagBlocksLowerTriangular" | custom-call | tf_op jit(solution)/shard_map/jit(_solve_triangular)/triangular_solve | solution.py:45
  879.9 134.3 %all-gather.14.cloned.1.call-done = bf16[64,60,256]{2,1,0:T(8,128)(2,1)} async-done(((bf16[1,60,256]{2,1,0:T(8,128)(2,1)}), bf16[64,60,256]{2,1,0:T(8,128)(2,1)}) %all-gather.14.cloned.1.call-update) | async-done | bytes 1966096 | tf_op jit(solution)/shard_map/all_gather | solution.py:50
  1014.2 2.5 reshape.305
  1018.3 4.1 neg.45
  1022.4 1.9 copy.139
  1024.3 2.1 neg.47
  1027.5 2.0 reshape.267
  1031.4 3.5 reshape.268
  (158 shorter events, 66.0 us)
Async XLA Ops:
  7.2 6.5 copy-start
  7.2 320.5 %all-gather.10.cloned.1.call-start = ((), (), s32[]{:S(2)}) async-start(), calls=%async_computation | async-start | bytes 2129920 | tf_op jit(solution)/shard_map/all_gather | solution.py:50
  8.5 5.2 collective-permute-start
  129.8 36.2 %copy-start.3 = (s32[2]{0:T(128)S(1)}, s32[2]{0:T(128)}, u32[]{:S(2)}) copy-start(s32[2]{0:T(128)} %iota_multiply_fusion) | copy-start | bytes 28
  191.1 479.6 %all-gather.12.cloned.1.call-start = ((), (), s32[]{:S(2)}) async-start(), calls=%async_computation.1 | async-start | bytes 2129920 | tf_op jit(solution)/shard_map/all_gather | solution.py:50
  347.8 16.5 %collective-permute-start.1 = (f32[60,3840]{1,0:T(8,128)S(1)}, f32[60,3840]{1,0:T(8,128)S(1)}, u32[]{:S(2)}, u32[]{:S(2)}) collective-permute-start(f32[60,3840]{1,0:T(8,128)S(1)} %reshape.248), channel_id=1, source_target_pairs={{0,128},{64,192},{128,0},{192,64},{256,384},{320,448},{384,256},{4... | collective-permute-start | bytes 2764808 | tf_op jit(solution)/shard_map/ppermute | solution.py:13
  534.8 479.4 %all-gather.14.cloned.1.call-start = ((), (), s32[]{:S(2)}) async-start(), calls=%async_computation.2 | async-start | bytes 2129920 | tf_op jit(solution)/shard_map/all_gather | solution.py:50
  687.9 7.7 copy-start.1
  690.7 18.0 %collective-permute-start.2 = (f32[60,3840]{1,0:T(8,128)S(1)}, f32[60,3840]{1,0:T(8,128)S(1)}, u32[]{:S(2)}, u32[]{:S(2)}) collective-permute-start(f32[60,3840]{1,0:T(8,128)S(1)} %reshape.259), channel_id=1, source_target_pairs={{0,256},{64,320},{128,384},{192,448},{256,0},{320,64},{384,128},{4... | collective-permute-start | bytes 2764808 | tf_op jit(solution)/shard_map/ppermute | solution.py:13
  733.7 82.7 %copy-start.2 = (pred[256,256]{1,0:T(8,128)(4,1)S(1)}, pred[256,256]{1,0:T(8,128)(4,1)}, u32[]{:S(2)}) copy-start(pred[256,256]{1,0:T(8,128)(4,1)} %copy.136) | copy-start | bytes 196612
Sparse Core Ops, SparseCore 0:
  191.2 136.4 all-gather.9
  534.9 135.7 all-gather.11
  878.4 135.7 all-gather.13
where the time goes:
time: 1050 us; the launch traced here: 1040 us
  waiting for transfers between devices  433 us (41%)
  blocking collectives  250 us (24%)
  other arithmetic  178 us (17%)
  local copies, waits for them, and re-layouts  111 us (11%)
  matrix products  41.4 us (4%)
  between operations  18.8 us (2%)
    all_gather x3, waiting for transfers between devices, factor_front(): lax.all_gather(rounded, 'front', axis=0, tiled=True)  407 us
    all_gather x3, blocking collectives, factor_front(): gathered = lax.all_gather(local_pivot, 'front', axis=0, tiled=True)  250 us
    another operation x20, other arithmetic, cholesky_lower(): return jnp.linalg.cholesky(symmetric)  103 us
    another operation x7, other arithmetic, factor_front(): solved = jax.scipy.linalg.solve_triangular(factor, lhs_rows.T, lower=True).T  60.4 us
    ppermute x3, waiting for transfers between devices, swapped(): return lax.ppermute(value, axis, pairs)  26.5 us
    neg x9, local copies, waits for them, and re-layouts, factor_front(): matrix = matrix.at[panel_rows:, last_col:].add(-reordered)  24.2 us
    reshape x6, local copies, waits for them, and re-layouts, scatter_rows(): grid = block.reshape(block_rows, devices, block_rows)  21.7 us
  transfers between devices with their start and end apart: 6, of which 5 were waited for; matrix products, arithmetic and copies ran while one was open for 1% of the time, Pallas kernels for 0%

commit v1 on v0

--- a/solution.py
+++ b/solution.py
@@ -47,7 +47,9 @@
     update = jnp.einsum(
         "ip,jp->ij",
         rounded,
-        lax.all_gather(rounded, "front", axis=0, tiled=True),
+        jnp.concatenate(
+            lax.all_to_all(jnp.stack([rounded] * lax.axis_size("front")), "front", 0, 0), axis=0
+        ),
         preferred_element_type=jnp.float32,
     )
     reordered = jnp.transpose(update.reshape(trailing, devices, trailing), (0, 2, 1)).reshape(

time: 1050 us -> 844 us (0.80)
  the two profiles are of different devices: /device:TPU:2 before, /device:TPU:4 now
where the time goes in v1:
time: 844 us; the launch traced here: 840 us
  blocking collectives  414 us (49%)
  other arithmetic  181 us (21%)
  local copies, waits for them, and re-layouts  90.1 us (11%)
  waiting for transfers between devices  81.1 us (10%)
  matrix products  53.3 us (6%)
  starting transfers between devices  13.1 us (2%)
    all_gather x3, blocking collectives, factor_front(): gathered = lax.all_gather(local_pivot, 'front', axis=0, tiled=True)  254 us
    all_to_all x2, blocking collectives, factor_front(): lax.all_to_all(jnp.stack([rounded] * lax.axis_size('front')), 'front', 0, 0)  161 us
    another operation x20, other arithmetic, cholesky_lower(): return jnp.linalg.cholesky(symmetric)  103 us
    another operation x7, other arithmetic, factor_front(): solved = jax.scipy.linalg.solve_triangular(factor, lhs_rows.T, lower=True).T  61.3 us
    all_to_all x1, waiting for transfers between devices, factor_front(): lax.all_to_all(jnp.stack([rounded] * lax.axis_size('front')), 'front', 0, 0)  53.6 us
    ppermute x3, waiting for transfers between devices, swapped(): return lax.ppermute(value, axis, pairs)  27.5 us
    dot_general x6, matrix products, scatter_rows(): placed = jnp.einsum('usb,ut->tsb', widened, table, precision=HIGH)  24.9 us
    reshape x6, local copies, waits for them, and re-layouts, scatter_rows(): grid = block.reshape(block_rows, devices, block_rows)  21.8 us
  transfers between devices with their start and end apart: 4, of which 4 were waited for; matrix products, arithmetic and copies ran while one was open for 1% of the time, Pallas kernels for 0%

profile of v1, /device:TPU:4, one launch (start us, length us, event | category | flops | bytes accessed | tf_op | source)
XLA Modules:
  0.0 839.9 jit_solution(9639115073263175992)
XLA Ops:
  2.0 1.9 collective-permute-start
  7.5 4.4 reshape.250
  12.0 2.9 convolution_bitcast_fusion.5
  14.9 2.4 fusion.10
  18.6 1.7 reshape.251
  20.3 2.9 reshape.252
  23.2 2.9 convolution_bitcast_fusion.4
  26.1 12.3 %fusion.8 = f32[64,64,64]{2,0,1:T(8,128)S(1)} fusion(f32[60,64,64]{2,1,0:T(8,128)S(1)} %convolution_bitcast_fusion.4, s32[60]{0:T(128)S(1)} %get-tuple-element.128), kind=kOutput, calls=%fused_computation.14 | convolution fusion | flops 188747520 | bytes 2031856 | tf_op jit(solution)/shard_map/usb,ut->tsb/dot_general | solution.py:25
  41.2 1.7 add_add_fusion.2
  42.9 88.9 %all-gather = f32[64,4,256]{2,1,0:T(4,128)S(1)} all-gather(f32[1,4,256]{2,1,0:T(4,128)S(1)} %slice_bitcast_fusion.17), channel_id=1, replica_groups=mesh['cube'=8,'front'=64] {'front'}, dimensions={0}, use_global_device_ids=true | all-gather | bytes 266240 | tf_op jit(solution)/shard_map/all_gather | solution.py:39
  132.4 11.7 %cholesky.172 = f32[128,128]{1,0:T(8,128)S(1)} custom-call(f32[128,128]{1,0:T(8,128)S(1)} %copy.106), custom_call_target="Cholesky" | custom-call | tf_op jit(solution)/shard_map/jit(cholesky)/cholesky | solution.py:31
  144.1 9.8 %custom-call.15 = f32[1,128,128]{1,2,0:T(8,128)S(1)} custom-call(f32[1,128,128]{2,1,0:T(8,128)S(1)} %get-tuple-element.119), custom_call_target="InvertDiagBlocksLowerTriangular" | custom-call | tf_op jit(solution)/shard_map/jit(cholesky)/cholesky | solution.py:31
  154.6 11.7 %cholesky.189 = f32[128,128]{1,0:T(8,128)S(1)} custom-call(f32[128,128]{1,0:T(8,128)S(1)} %copy.108), custom_call_target="Cholesky" | custom-call | tf_op jit(solution)/shard_map/jit(cholesky)/cholesky | solution.py:31
  169.3 4.5 while.9
  173.8 19.7 %custom-call.16 = f32[2,128,128]{1,2,0:T(8,128)S(1)} custom-call(f32[2,128,128]{2,1,0:T(8,128)S(1)} %get-tuple-element.60), custom_call_target="InvertDiagBlocksLowerTriangular" | custom-call | tf_op jit(solution)/shard_map/jit(_solve_triangular)/triangular_solve | solution.py:45
  194.4 91.0 %all_to_all.15 = bf16[64,60,256]{2,1,0:T(8,128)(2,1)S(1)} all-to-all(bf16[64,60,256]{2,1,0:T(8,128)(2,1)S(1)} %stack.15), channel_id=1, replica_groups=mesh['cube'=8,'front'=64] {'front'}, dimensions={0} | all-to-all | bytes 3932160 | tf_op jit(solution)/shard_map/all_to_all | solution.py:51
  285.4 2.4 negate_bitcast_fusion.2
  290.5 2.2 slice_add_fusion.2
  292.8 2.0 reshape.259
  294.8 1.9 copy.113
  296.6 2.8 reshape.260
  299.5 3.1 collective-permute-start.1
  303.0 12.5 %collective-permute-done.1 = f32[60,3840]{1,0:T(8,128)S(1)} collective-permute-done((f32[60,3840]{1,0:T(8,128)S(1)}, f32[60,3840]{1,0:T(8,128)S(1)}, u32[]{:S(2)}, u32[]{:S(2)}) %collective-permute-start.1) | collective-permute-done | bytes 921632 | tf_op jit(solution)/shard_map/ppermute | solution.py:13
  316.9 4.2 reshape.261
  321.2 2.9 convolution_bitcast_fusion.3
  324.1 2.4 fusion.6
  329.4 2.9 reshape.263
  332.3 2.9 convolution_bitcast_fusion.2
  335.3 2.8 fusion.4
  339.3 1.7 reshape.264
  342.7 81.3 %all-gather.1 = f32[64,4,256]{2,1,0:T(4,128)S(1)} all-gather(f32[1,4,256]{2,1,0:T(4,128)S(1)} %slice_bitcast_fusion.16), channel_id=1, replica_groups=mesh['cube'=8,'front'=64] {'front'}, dimensions={0}, use_global_device_ids=true | all-gather | bytes 266240 | tf_op jit(solution)/shard_map/all_gather | solution.py:39
  424.6 11.7 %cholesky.206 = f32[128,128]{1,0:T(8,128)S(1)} custom-call(f32[128,128]{1,0:T(8,128)S(1)} %copy.122), custom_call_target="Cholesky" | custom-call | tf_op jit(solution)/shard_map/jit(cholesky)/cholesky | solution.py:31
  437.0 9.8 %custom-call.17 = f32[1,128,128]{1,2,0:T(8,128)S(1)} custom-call(f32[1,128,128]{2,1,0:T(8,128)S(1)} %get-tuple-element.115), custom_call_target="InvertDiagBlocksLowerTriangular" | custom-call | tf_op jit(solution)/shard_map/jit(cholesky)/cholesky | solution.py:31
  447.5 11.7 %cholesky.223 = f32[128,128]{1,0:T(8,128)S(1)} custom-call(f32[128,128]{1,0:T(8,128)S(1)} %copy.124), custom_call_target="Cholesky" | custom-call | tf_op jit(solution)/shard_map/jit(cholesky)/cholesky | solution.py:31
  462.0 4.3 while.10
  466.3 19.7 %custom-call.18 = f32[2,128,128]{1,2,0:T(8,128)S(1)} custom-call(f32[2,128,128]{2,1,0:T(8,128)S(1)} %get-tuple-element.61), custom_call_target="InvertDiagBlocksLowerTriangular" | custom-call | tf_op jit(solution)/shard_map/jit(_solve_triangular)/triangular_solve | solution.py:45
  486.9 69.7 %all_to_all.16 = bf16[64,60,256]{2,1,0:T(8,128)(2,1)S(1)} all-to-all(bf16[64,60,256]{2,1,0:T(8,128)(2,1)S(1)} %stack.17), channel_id=1, replica_groups=mesh['cube'=8,'front'=64] {'front'}, dimensions={0} | all-to-all | bytes 3932160 | tf_op jit(solution)/shard_map/all_to_all | solution.py:51
  556.6 2.4 negate_bitcast_fusion.1
  561.7 2.2 slice_add_fusion.1
  563.9 2.0 reshape.270
  566.0 1.9 copy.129
  567.8 2.8 reshape.271
  570.7 2.4 collective-permute-start.2
  573.7 14.5 %collective-permute-done.2 = f32[60,3840]{1,0:T(8,128)S(1)} collective-permute-done((f32[60,3840]{1,0:T(8,128)S(1)}, f32[60,3840]{1,0:T(8,128)S(1)}, u32[]{:S(2)}, u32[]{:S(2)}) %collective-permute-start.2) | collective-permute-done | bytes 921632 | tf_op jit(solution)/shard_map/ppermute | solution.py:13
  589.6 4.5 reshape.272
  594.1 2.9 convolution_bitcast_fusion.1
  597.0 2.4 fusion.2
  602.3 2.9 reshape.274
  605.2 2.9 convolution_bitcast_fusion
  608.2 2.6 fusion
  612.0 1.7 reshape.275
  615.4 83.2 %all-gather.2 = f32[64,4,256]{2,1,0:T(4,128)S(1)} all-gather(f32[1,4,256]{2,1,0:T(4,128)S(1)} %slice_bitcast_fusion.15), channel_id=1, replica_groups=mesh['cube'=8,'front'=64] {'front'}, dimensions={0}, use_global_device_ids=true | all-gather | bytes 266240 | tf_op jit(solution)/shard_map/all_gather | solution.py:39
  699.1 11.7 %cholesky.240 = f32[128,128]{1,0:T(8,128)S(1)} custom-call(f32[128,128]{1,0:T(8,128)S(1)} %cholesky.276), custom_call_target="Cholesky" | custom-call | tf_op jit(solution)/shard_map/jit(cholesky)/cholesky | solution.py:31
  711.4 9.8 %custom-call.19 = f32[1,128,128]{1,2,0:T(8,128)S(1)} custom-call(f32[1,128,128]{2,1,0:T(8,128)S(1)} %get-tuple-element.111), custom_call_target="InvertDiagBlocksLowerTriangular" | custom-call | tf_op jit(solution)/shard_map/jit(cholesky)/cholesky | solution.py:31
  721.8 11.7 %cholesky.257 = f32[128,128]{1,0:T(8,128)S(1)} custom-call(f32[128,128]{1,0:T(8,128)S(1)} %convolution_subtract_fusion), custom_call_target="Cholesky" | custom-call | tf_op jit(solution)/shard_map/jit(cholesky)/cholesky | solution.py:31
  736.3 4.3 while.11
  740.6 19.7 %custom-call.20 = f32[2,128,128]{1,2,0:T(8,128)S(1)} custom-call(f32[2,128,128]{2,1,0:T(8,128)S(1)} %get-tuple-element.62), custom_call_target="InvertDiagBlocksLowerTriangular" | custom-call | tf_op jit(solution)/shard_map/jit(_solve_triangular)/triangular_solve | solution.py:45
  762.6 5.7 all-to-all-start.2
  771.3 53.6 %all-to-all-done.2 = bf16[64,60,256]{2,1,0:T(8,128)(2,1)S(1)} async-done(((bf16[64,60,256]{2,1,0:T(8,128)(2,1)}), bf16[64,60,256]{2,1,0:T(8,128)(2,1)S(1)}, u32[]{:S(2)}, u32[]{:S(2)}) %all-to-all-start.2) | async-done | bytes 1966112 | tf_op jit(solution)/shard_map/all_to_all | solution.py:51
  824.9 2.4 negate_bitcast_fusion
  830.0 2.2 slice_add_fusion
  832.2 2.0 reshape.279
  834.3 1.9 copy.140
  836.1 3.5 reshape.280
  (148 shorter events, 60.5 us)
Async XLA Ops:
  0.6 5.8 copy-start.2
  2.0 4.5 collective-permute-start
  299.5 16.0 %collective-permute-start.1 = (f32[60,3840]{1,0:T(8,128)S(1)}, f32[60,3840]{1,0:T(8,128)S(1)}, u32[]{:S(2)}, u32[]{:S(2)}) collective-permute-start(f32[60,3840]{1,0:T(8,128)S(1)} %reshape.260), channel_id=1, source_target_pairs={{0,128},{64,192},{128,0},{192,64},{256,384},{320,448},{384,256},{4... | collective-permute-start | bytes 2764808 | tf_op jit(solution)/shard_map/ppermute | solution.py:13
  327.7 1.7 copy-start
  570.7 17.5 %collective-permute-start.2 = (f32[60,3840]{1,0:T(8,128)S(1)}, f32[60,3840]{1,0:T(8,128)S(1)}, u32[]{:S(2)}, u32[]{:S(2)}) collective-permute-start(f32[60,3840]{1,0:T(8,128)S(1)} %reshape.271), channel_id=1, source_target_pairs={{0,256},{64,320},{128,384},{192,448},{256,0},{320,64},{384,128},{4... | collective-permute-start | bytes 2764808 | tf_op jit(solution)/shard_map/ppermute | solution.py:13
  600.7 1.7 copy-start.1
  762.6 62.4 %all-to-all-start.2 = ((bf16[64,60,256]{2,1,0:T(8,128)(2,1)}), bf16[64,60,256]{2,1,0:T(8,128)(2,1)S(1)}, u32[]{:S(2)}, u32[]{:S(2)}) async-start(bf16[64,60,256]{2,1,0:T(8,128)(2,1)} %stack.20), calls=%async_computation.2 | async-start | bytes 4194304 | tf_op jit(solution)/shard_map/all_to_all | solution.py:51
